TPU v7x, 512 devices: a whole 4x4x16 slice. The times are simulated.
512 devices in a mesh: dp: 64 (over z_lo, y, core), tensor: 8 (over x, z_hi).
Axes of the slice: x: 4, y: 4, z: 16 (z_hi: 2, z_lo: 8; z = z_hi * 8 + z_lo), core: 2. Of those that a mesh axis runs over, the one named last changes fastest.
Arguments:
- inputs: bfloat16 [8192, 8192], P('dp'), may hold values from -6 to 6
- weight_blocks: bfloat16 [112, 4096, 128], P('tensor', 'dp'), may hold values from -0.09375 to 0.09375
- block_rows: int32 [112, 32], P('tensor'), may hold values from 0 to 63, as said below
- grad_hidden: bfloat16 [8192, 14336], P('dp', 'tensor'), may hold values from -6 to 6
- projection: bfloat16 [64, 8192], replicated, may hold values from -0.0009765625 to 0.0009765625
- momentum: float32 [64, 14336], P('dp', 'tensor'), may hold values from -6 to 6
Outputs:
- hidden: bfloat16 [8192, 14336], P('dp', 'tensor')
- input_grad: bfloat16 [8192, 8192], P('dp', 'tensor')
- new_momentum: float32 [64, 14336], P('dp', 'tensor')
Inputs may be any that keep to these rules, and one draw needn't show every extreme that they name: `block_rows`: the 32 entries of a row are different block rows. Block columns 2j and 2j + 1 together name every block row exactly once.
All inputs are finite; a program needn't handle non-finite values.
Results may differ from a plain program's by a relative error of at most 0.015.
Values may be sent and summed in bfloat16 or wider, within the bound.
No kernel may reach another device: no remote copies, remote signals or barrier semaphores. Data moves between devices by JAX's collectives and lax.ppermute only.
A program may use at most 128 MiB of HBM per device.

v0:
```python
import jax
import jax.numpy as jnp
from jax import lax
from jax.sharding import PartitionSpec as P


def body(inputs, weight_blocks, block_rows, grad_hidden, projection, momentum):
    rows_here = inputs.shape[0]
    model_width = inputs.shape[1]
    panels = block_rows.shape[0]
    kept_slots = block_rows.shape[1]
    block_size = weight_blocks.shape[2]
    rank_size = projection.shape[0]
    row_blocks = model_width // block_size
    gathered = lax.all_gather(weight_blocks, "dp", axis=1, tiled=True)
    input_blocks = inputs.reshape(rows_here, row_blocks, block_size)
    proj_blocks = projection.reshape(rank_size, row_blocks, block_size)
    grad_panels = grad_hidden.reshape(rows_here, panels, block_size).transpose(1, 0, 2)

    def panel_turn(grads_acc, items):
        rows_now, panel_weights, panel_grads = items
        picked = jnp.take(input_blocks, rows_now, axis=1).reshape(
            rows_here, kept_slots * block_size
        )
        hidden_panel = jnp.dot(picked, panel_weights, preferred_element_type=jnp.float32).astype(
            jnp.bfloat16
        )
        contribution = jnp.dot(panel_grads, panel_weights.T, preferred_element_type=jnp.float32)
        contribution = contribution.reshape(rows_here, kept_slots, block_size)
        grads_acc = grads_acc.at[:, rows_now].add(contribution)
        chosen = jnp.take(proj_blocks, rows_now, axis=1).reshape(rank_size, kept_slots * block_size)
        projected = jnp.dot(chosen, picked.T, preferred_element_type=jnp.float32)
        compressed_panel = jnp.dot(
            projected, panel_grads.astype(jnp.float32), precision=lax.Precision.HIGHEST
        )
        return (grads_acc, (hidden_panel, compressed_panel))

    start_acc = jnp.zeros((rows_here, row_blocks, block_size), jnp.float32)
    grads_acc, (hidden_parts, compressed_parts) = lax.scan(
        panel_turn, start_acc, (block_rows, gathered, grad_panels)
    )
    hidden = hidden_parts.transpose(1, 0, 2).reshape(rows_here, panels * block_size)
    input_grad = lax.psum_scatter(
        grads_acc.reshape(rows_here, model_width).astype(jnp.bfloat16),
        "tensor",
        scatter_dimension=1,
        tiled=True,
    )
    compressed = compressed_parts.transpose(1, 0, 2).reshape(rank_size, panels * block_size)
    summed = lax.psum_scatter(compressed, "dp", scatter_dimension=0, tiled=True)
    new_momentum = 0.9 * momentum + summed
    return (hidden, input_grad, new_momentum)


def solution(mesh):
    placed = (
        P("dp", None),
        P("tensor", "dp", None),
        P("tensor", None),
        P("dp", "tensor"),
        P(),
        P("dp", "tensor"),
    )
    return jax.shard_map(
        body,
        mesh=mesh,
        in_specs=placed,
        out_specs=(P("dp", "tensor"), P("dp", "tensor"), P("dp", "tensor")),
        check_vma=False,
    )
```

profile of v0, /device:TPU:8, one launch (start us, length us, event | category | flops | bytes accessed | tf_op | source)
XLA Modules:
  0.0 1452.0 jit_solution(14074415547483584652)
XLA Ops:
  8.0 3.2 copy.30
  11.2 2.9 copy.32
  17.4 132.0 %all-gather.2.cloned.1.call-done = bf16[14,4096,128]{2,1,0:T(8,128)(2,1)} async-done(((bf16[14,64,128]{2,1,0:T(8,128)(2,1)}), bf16[14,4096,128]{2,1,0:T(8,128)(2,1)}) %all-gather.2.cloned.1.call-update) | async-done | bytes 14680080 | tf_op jit(solution)/shard_map/all_gather | solution.py:15
  151.9 328.4 %while.14 = (s32[]{:T(128)}, f32[128,64,128]{2,0,1:T(8,128)}, bf16[14,128,128]{1,2,0:T(8,128)(2,1)}, f32[14,64,128]{2,1,0:T(8,128)}, s32[14,32]{1,0:T(8,128)}, /...) while((s32[]{:T(128)}, f32[128,64,128]{2,0,1:T(8,128)}, ...), condition=%wide.region_2.3_spmd, body=%wide.region_0.2_spmd.sunk | while | flops 349979936 | bytes 27073644 | solution.py:39
  159.9 2.6 gather_fusion.1
  168.2 7.1 scatter_fusion
  183.4 2.6 gather_fusion.1
  191.7 7.1 scatter_fusion
  206.8 2.6 gather_fusion.1
  215.2 7.1 scatter_fusion
  230.3 2.6 gather_fusion.1
  238.6 7.1 scatter_fusion
  253.8 2.6 gather_fusion.1
  262.1 7.1 scatter_fusion
  277.3 2.6 gather_fusion.1
  285.6 7.1 scatter_fusion
  309.1 7.1 scatter_fusion
  324.2 2.6 gather_fusion.1
  332.5 7.1 scatter_fusion
  347.6 2.6 gather_fusion.1
  355.9 7.1 scatter_fusion
  371.1 2.6 gather_fusion.1
  379.4 7.1 scatter_fusion
  394.5 2.6 gather_fusion.1
  402.9 7.1 scatter_fusion
  418.0 2.6 gather_fusion.1
  426.3 7.1 scatter_fusion
  449.7 7.1 scatter_fusion
  473.2 7.1 scatter_fusion
  482.1 3.8 copy_bitcast_fusion
  488.3 803.9 %all-reduce.3.cloned.1.call-done = f32[64,1792]{1,0:T(8,128)} async-done(((f32[64,1792]{1,0:T(8,128)}), f32[64,1792]{1,0:T(8,128)}) %all-reduce.3.cloned.1.call-update) | async-done | bytes 458768
  1294.2 151.3 %reduce-scatter.2.cloned.1.call-done = bf16[128,1024]{1,0:T(8,128)(2,1)} async-done(((bf16[128,8192]{1,0:T(8,128)(2,1)}), bf16[128,1024]{1,0:T(8,128)(2,1)}) %reduce-scatter.2.cloned.1.call-update) | async-done | bytes 262160 | tf_op jit(solution)/shard_map/reduce_scatter | solution.py:43
  (234 shorter events, 212.0 us)
Async XLA Ops:
  7.2 9.0 copy-start
  7.2 142.2 %all-gather.2.cloned.1.call-start = ((), (), s32[]{:S(2)}) async-start(), calls=%async_computation.1 | async-start | bytes 14909440 | tf_op jit(solution)/shard_map/all_gather | solution.py:15
  7.9 1284.3 %all-reduce.3.cloned.1.call-start = ((), (), s32[]{:S(2)}) async-start(), calls=%async_computation.3 | async-start | bytes 917504
  157.1 1.5 copy-start.1
  180.6 1.5 copy-start.1
  204.1 1.5 copy-start.1
  227.5 1.5 copy-start.1
  251.0 1.5 copy-start.1
  274.5 1.5 copy-start.1
  298.0 1.5 copy-start.1
  321.4 1.5 copy-start.1
  344.8 1.5 copy-start.1
  368.3 1.5 copy-start.1
  391.8 1.5 copy-start.1
  415.2 1.5 copy-start.1
  438.6 1.5 copy-start.1
  462.1 1.5 copy-start.1
  482.1 963.4 %reduce-scatter.2.cloned.1.call-start = ((), (), s32[]{:S(2)}) async-start(), calls=%async_computation.2 | async-start | bytes 2359296 | tf_op jit(solution)/shard_map/reduce_scatter | solution.py:43
  486.0 1.3 copy-start.2
  486.0 806.2 %copy-start.3 = (f32[1,1792]{1,0:T(1,128)S(1)}, f32[1,1792]{1,0:T(1,128)}, u32[]{:S(2)}) copy-start(f32[1,1792]{1,0:T(1,128)} %param.13) | copy-start | bytes 21508
Sparse Core Ops, SparseCore 0:
  10.2 139.1 all-gather.1
  482.2 809.9 all-reduce.2
  1298.1 147.3 reduce-scatter.1
where the time goes:
time: 1460 us; the launch traced here: 1450 us
  waiting for transfers between devices  1090 us (75%)
  local copies, waits for them, and re-layouts  136 us (9%)
  other arithmetic  127 us (9%)
  matrix products  86.2 us (6%)
    unnamed x4, waiting for transfers between devices  805 us
    reduce_scatter x1, waiting for transfers between devices, body(): lax.psum_scatter(grads_acc.reshape(rows_here, model_width).astype(jnp.bfl...  151 us
    all_gather x1, waiting for transfers between devices, body(): gathered = lax.all_gather(weight_blocks, 'dp', axis=1, tiled=True)  132 us
    scatter-add x14, other arithmetic, panel_turn(): grads_acc = grads_acc.at[:, rows_now].add(contribution)  99.5 us
    gather x14, local copies, waits for them, and re-layouts, panel_turn(): jnp.take(proj_blocks, rows_now, axis=1)  36.9 us
    dot_general x14, matrix products, panel_turn(): jnp.dot(panel_grads, panel_weights.T, preferred_element_type=jnp.float32)  35.5 us
    gather x14, local copies, waits for them, and re-layouts, panel_turn(): jnp.take(input_blocks, rows_now, axis=1)  32.7 us
  transfers between devices with their start and end apart: 3, of which 3 were waited for; matrix products, arithmetic and copies ran while one was open for 1% of the time, Pallas kernels for 0%

commit v1 on v0

v1 whole, which is shorter than its diff:
```python
import functools

import jax
import jax.numpy as jnp
from jax import lax
from jax.experimental import pallas as pl
from jax.experimental.pallas import tpu as pltpu
from jax.sharding import PartitionSpec as P

PARTS = 2
Z, Y, C = 8, 4, 2
X, H = 4, 2
F32, BF16 = jnp.float32, jnp.bfloat16
NT = (((1,), (1,)), ((), ()))


def place(z, y, core):
    return (z * Y + y) * C + core


def every(order):
    return [order(z, y, core) for z in range(Z) for y in range(Y) for core in range(C)]


def flipped(bits):
    return every(lambda z, y, core: (place(z, y, core), place(z ^ (bits // Y), y ^ (bits % Y), core)))


OTHER_CORE = every(lambda z, y, core: (place(z, y, core), place(z, y, 1 - core)))
Z_STEPS = (16, 8, 4)
Y_STEPS = ((1, 3), (3, 1))
X_RINGS = [[x * H + h for x in range(X)] for h in range(H)]
CORNERS = [
    [place(z, y, core) * (X * H) + x * H + h for h in range(H) for core in range(C)]
    for z in range(Z)
    for y in range(Y)
    for x in range(X)
]


def corner(far_h, far_core):
    return [(i, i ^ (far_core * X * H + far_h)) for i in range(Z * Y * C * X * H)]


def after(value, *earlier):
    for e in earlier:
        value = value + jnp.minimum(jnp.abs(e[(0,) * e.ndim]), 0).astype(value.dtype)
    return value


def params(**more):
    return pltpu.CompilerParams(vmem_limit_bytes=50 * 1024 * 1024, **more)


def cost(flops, moved):
    return pl.CostEstimate(flops=flops, bytes_accessed=moved, transcendentals=0)


def regroup(width, parts, half):
    rows = half // parts
    column = lax.broadcasted_iota(jnp.int32, (1, width), 1)
    block, inside = column // (2 * half), column % (2 * half)
    side, deep = inside // half, inside % half
    part, row = deep // rows, deep % rows
    blocks = width // (2 * half)
    source = ((side * parts + part) * blocks + block) * rows + row
    here = lax.broadcasted_iota(jnp.int32, (width, width), 0)
    return jnp.where(here == source, 1.0, 0.0).astype(BF16)


def split_kernel(parts, half, who, x_ref, p_ref, keep_ref, send_ref, proj_ref, order):
    core = who[0]
    width = order.shape[0]
    piece = width // (2 * parts)
    full = keep_ref.shape[1] // parts
    order[...] = regroup(width, parts, half)
    groups = x_ref.shape[1] // width

    def mix(ref):
        stacked = jnp.concatenate([ref[:, g * width : (g + 1) * width] for g in range(groups)], axis=0)
        return lax.dot_general(stacked, order[...], NT, preferred_element_type=F32).astype(BF16)

    x_mixed, p_mixed = mix(x_ref), mix(p_ref)

    def deal(mixed, ref, side):
        rows = ref.shape[0]
        for g in range(groups):
            for p in range(parts):
                to = slice(p * full + g * piece, p * full + (g + 1) * piece)
                at = (side * parts + p) * piece
                ref[:, to] = mixed[g * rows : (g + 1) * rows, at : at + piece]

    for value in range(C):

        @pl.when(core == value)
        def _(value=value):
            deal(x_mixed, keep_ref, value)
            deal(x_mixed, send_ref, 1 - value)
            deal(p_mixed, proj_ref, value)


def compress_kernel(xk_ref, xr_ref, gk_ref, gr_ref, proj_ref, mask_ref, out_ref, masked):
    rank = proj_ref.shape[0]
    pairs = mask_ref.shape[0]
    side = 2 * mask_ref.shape[0]
    block = gk_ref.shape[1] // side
    for j in range(pairs):
        masked[j * rank : (j + 1) * rank, :] = proj_ref[...] * mask_ref[j : j + 1, :]
    masked[pairs * rank : (pairs + 1) * rank, :] = proj_ref[...]
    held = []
    for x_ref in (xk_ref, xr_ref):
        held.append(lax.dot_general(masked[...], x_ref[...], NT, preferred_element_type=F32))
    for panel in range(side):
        total = None
        for seen, g_ref in zip(held, (gk_ref, gr_ref)):
            j = panel // 2
            part = seen[j * rank : (j + 1) * rank, :]
            if panel % 2:
                part = seen[pairs * rank :, :] - part
            high = part.astype(BF16)
            low = (part - high.astype(F32)).astype(BF16)
            grads = g_ref[:, panel * block : (panel + 1) * block]
            term = jnp.dot(high, grads, preferred_element_type=F32) + jnp.dot(low, grads, preferred_element_type=F32)
            total = term if total is None else total + term
        out_ref[:, panel, :] = total


def main_kernel(first, last, who, rows_ref, *rest):
    rest = list(rest)
    chunks = [rest.pop(0) for _ in range(4 if first else 1)]
    xk_ref, xr_ref, gk_ref, gr_ref = (rest.pop(0) for _ in range(4))
    acc_k, acc_r = (None, None) if first else (rest.pop(0), rest.pop(0))
    grad_ref, hk_ref, hr_ref, dense = rest
    core, mine = who[0], who[1]
    deep, block = chunks[0].shape[-2:]
    panels = rows_ref.shape[0]
    some = panels // 2
    tokens = xk_ref.shape[0]
    blank = jnp.zeros((deep, block), BF16)

    def lay(panel, slot, weights):
        at = pl.multiple_of(rows_ref[panel, slot] * deep, deep)
        other = panel ^ 1
        dense[pl.ds(at, deep), panel * block : (panel + 1) * block] = weights
        dense[pl.ds(at, deep), other * block : (other + 1) * block] = blank

    def put(slot, carry):
        for panel in range(panels):
            lay(panel, slot, chunks[0][panel, slot, core])
        return carry

    def put_steps(i, carry):
        for q, (y_first, y_second) in enumerate(Y_STEPS):
            for late in range(2):
                far = (i // 8) * y_first ^ late * y_second
                slot = mine ^ far ^ ((i // 4) % 2 * Z_STEPS[2]) ^ ((i // 2) % 2 * Z_STEPS[1]) ^ (i % 2 * Z_STEPS[0])
                for n in range(some):
                    lay(q * some + n, slot, chunks[2 * q + late][i, n])
        return carry

    if first:
        lax.fori_loop(0, chunks[0].shape[0], put_steps, 0)
    else:
        lax.fori_loop(0, chunks[0].shape[1], put, 0)
    share = dense.shape[0] // (X * H)
    for x in range(X):
        tile = dense[x * H * share : (x + 1) * H * share, :]
        for t, g_ref in enumerate((gk_ref, gr_ref)):
            out = lax.dot_general(g_ref[...], tile, NT, preferred_element_type=F32).astype(BF16)
            for h in range(H):
                grad_ref[x, h, t * tokens : (t + 1) * tokens, :] = out[:, h * share : (h + 1) * share]
    step = 2 * block
    for n in range(panels // 2):
        cols = slice(n * step, (n + 1) * step)
        for x_ref, h_ref, acc in ((xk_ref, hk_ref, acc_k), (xr_ref, hr_ref, acc_r)):
            out = jnp.dot(x_ref[...], dense[:, cols], preferred_element_type=F32)
            if acc is not None:
                out = out + acc[:, cols]
            h_ref[:, cols] = out.astype(h_ref.dtype)


def reduce_kernel(near, who, r_ref, *outs):
    core, h_here = who[0], who[2]
    tokens = outs[0].shape[-2]
    for far_h in range(H):
        for side in range(C):
            at = pl.ds(side * tokens, tokens) if near else pl.ds(pl.multiple_of((side ^ core) * tokens, tokens), tokens)
            h = h_here ^ far_h if near else far_h
            total = r_ref[0, h, at, :].astype(F32)
            for x in range(1, X):
                total = total + r_ref[x, h, at, :].astype(F32)
            if near:
                outs[far_h * C + side][...] = total.astype(BF16)
            else:
                outs[0][far_h * C + side] = total.astype(BF16)


def final_kernel(parts, half, who, *refs):
    near, (r,), out_ref = refs[:4], refs[4:-1], refs[-1]
    width = out_ref.shape[1]
    mine = near[0][...].astype(F32) + near[2][...].astype(F32)
    other = near[1][...].astype(F32) + near[3][...].astype(F32)
    columns = []
    for side in range(C):
        columns.append(jnp.where(who[0] == side, mine, other).astype(BF16))
        columns.append((r[side].astype(F32) + r[C + side].astype(F32)).astype(BF16))
    piece = 128
    group = 2 * parts * piece
    order = regroup(group, parts, half)
    for g in range(width // group):
        together = jnp.concatenate([c[:, g * piece : (g + 1) * piece] for c in columns], axis=1)
        out_ref[:, g * group : (g + 1) * group] = jnp.dot(together, order, preferred_element_type=F32).astype(BF16)


def body(inputs, weight_blocks, block_rows, grad_hidden, projection, momentum):
    tokens, width = inputs.shape
    panels, half, block = weight_blocks.shape
    slots = block_rows.shape[1]
    rank = projection.shape[0]
    row_blocks = width // block
    parts, deep = PARTS, half // PARTS
    units = grad_hidden.shape[1]
    here = lax.axis_index("dp")
    who = jnp.stack([here % C, here // C, lax.axis_index("tensor") % H]).astype(jnp.int32)
    smem = pl.BlockSpec(memory_space=pltpu.SMEM)
    vmem = pl.BlockSpec(memory_space=pltpu.VMEM)
    sds = jax.ShapeDtypeStruct

    keep, send, proj = pl.pallas_call(
        functools.partial(split_kernel, parts, half),
        out_shape=(sds((tokens, width // 2), BF16), sds((tokens, width // 2), BF16), sds((rank, width // 2), BF16)),
        in_specs=[smem, vmem, vmem],
        out_specs=(vmem, vmem, vmem),
        scratch_shapes=[pltpu.VMEM((2 * parts * block, 2 * parts * block), BF16)],
        compiler_params=params(),
        cost_estimate=cost(4 * 10**9, 6 * 10**6),
        name="split",
    )(who, inputs, projection)
    received = lax.ppermute(send, "dp", OTHER_CORE)
    grads_received = lax.ppermute(grad_hidden, "dp", OTHER_CORE)

    named = (block_rows[0::2, :, None] == jnp.arange(row_blocks, dtype=jnp.int32)).any(axis=1)
    mask = jnp.tile(jnp.repeat(named, deep, axis=1), (1, parts)).astype(BF16)
    def compress(first_seen, second_seen):
        out = pl.pallas_call(
            compress_kernel,
            out_shape=sds((rank, panels, block), F32),
            in_specs=[vmem] * 6,
            out_specs=vmem,
            scratch_shapes=[pltpu.VMEM(((panels // 2 + 1) * rank, width // 2), BF16)],
            compiler_params=params(),
            cost_estimate=cost(4 * 10**9, 6 * 10**6),
            name="compress",
        )(keep, received, grad_hidden, grads_received, proj, after(mask, first_seen))
        return out, lax.all_to_all(after(out, second_seen), "dp", 0, 0, tiled=True).sum(axis=0)

    finals, crossings, acc = [], [], ()
    whole = lambda *shape: pl.BlockSpec(shape, lambda i: (0,) * len(shape))
    for p in range(parts):
        own = weight_blocks[:, p * deep : (p + 1) * deep]
        if p == 0:
            chunks, seen = own[None], []
            for step in Z_STEPS:
                if step == Z_STEPS[2]:
                    compressed, summed = compress(*seen)
                    chunks = after(chunks, compressed)
                far = lax.ppermute(chunks, "dp", flipped(step))
                seen.append(far)
                chunks = jnp.concatenate([chunks, far])
            gathered = []
            for q, (y_first, y_second) in enumerate(Y_STEPS):
                some = chunks[:, q * (panels // 2) : (q + 1) * (panels // 2)]
                some = jnp.concatenate([some, lax.ppermute(some, "dp", flipped(y_first))])
                gathered += [some, lax.ppermute(some, "dp", flipped(y_second))]
            shapes = [whole(16, panels // 2, deep, block)] * 4
        else:
            gathered = [lax.all_gather(own, "dp", axis=1, tiled=True).reshape(panels, slots, C, deep, block)]
            shapes = [whole(panels, slots, C, deep, block)]
        turn = after(who, crossed) if p else after(who, summed)
        first, last = p == 0, p == parts - 1
        part_spec = pl.BlockSpec((tokens, row_blocks * deep), lambda i, p=p: (0, p))
        h_types = (F32, BF16 if last else F32)
        share = 8 * deep
        grad, *acc = pl.pallas_call(
            functools.partial(main_kernel, first, last),
            grid=(1,),
            out_shape=(
                sds((X, H, 2 * tokens, share), BF16),
                sds((tokens, units), h_types[0]),
                sds((tokens, units), h_types[1]),
            ),
            in_specs=[smem, smem, *shapes, part_spec, part_spec]
            + [whole(tokens, units)] * (2 if first else 4),
            out_specs=(whole(X, H, 2 * tokens, share), whole(tokens, units), whole(tokens, units)),
            scratch_shapes=[pltpu.VMEM((row_blocks * deep, units), BF16)],
            compiler_params=params(),
            cost_estimate=cost(8 * 10**9 // parts, 8 * 10**6),
            name="main",
        )(turn, block_rows, *gathered, keep, received, grad_hidden, grads_received, *acc)
        crossed = lax.all_to_all(grad, "tensor", 0, 0, tiled=True, axis_index_groups=X_RINGS)
        crossings.append(crossed)
    for p in range(parts):
        near = p == 0
        piece = sds((tokens, share), BF16)
        out = pl.pallas_call(
            functools.partial(reduce_kernel, near),
            out_shape=(piece,) * 4 if near else (sds((H * C, tokens, share), BF16),),
            in_specs=[smem, vmem],
            out_specs=(vmem,) * (4 if near else 1),
            compiler_params=params(),
            cost_estimate=cost(10**6, 10**6),
            name="reduce",
        )(after(who, *finals[1:]) if p else after(who, grad), crossings[p])
        reduced = out[0]
        if near:
            finals = [out[0]] + [lax.ppermute(out[i], ("dp", "tensor"), corner(i // C, i % C)) for i in range(1, 4)]
        else:
            finals.append(lax.all_to_all(reduced, ("dp", "tensor"), 0, 0, tiled=True, axis_index_groups=CORNERS))
    hidden_received = lax.ppermute(acc[1], "dp", OTHER_CORE)
    hidden = (acc[0] + hidden_received.astype(F32)).astype(BF16)
    new_momentum = 0.9 * momentum + summed.reshape(1, units)
    input_grad = pl.pallas_call(
        functools.partial(final_kernel, parts, half),
        out_shape=sds((tokens, width // (X * H)), BF16),
        in_specs=[smem] + [vmem] * 5,
        out_specs=vmem,
        compiler_params=params(),
        cost_estimate=cost(10**8, 10**6),
        name="final",
    )(who, *finals)
    return hidden, input_grad, new_momentum


def solution(mesh):
    placed = (
        P("dp", None),
        P("tensor", "dp", None),
        P("tensor", None),
        P("dp", "tensor"),
        P(),
        P("dp", "tensor"),
    )
    return jax.shard_map(
        body,
        mesh=mesh,
        in_specs=placed,
        out_specs=(P("dp", "tensor"), P("dp", "tensor"), P("dp", "tensor")),
        check_vma=False,
    )
```

time: 1460 us -> 251 us (0.17)
  the two profiles are of different devices: /device:TPU:8 before, /device:TPU:123 now
where the time goes in v1:
time: 251 us; the launch traced here: 250 us
  starting transfers between devices  88.6 us (35%)
  waiting for transfers between devices  71.8 us (29%)
  Pallas kernels  33.7 us (13%)
  between operations  20.1 us (8%)
  local copies, waits for them, and re-layouts  19.5 us (8%)
  blocking collectives  12.8 us (5%)
  other arithmetic  3.18 us (1%)
    pallas_call x2, Pallas kernels, body(): pl.pallas_call(functools.partial(main_kernel, first, last), grid=(1,), ou...  22.8 us
    ppermute x2, waiting for transfers between devices, body(): gathered += [some, lax.ppermute(some, 'dp', flipped(y_second))]  22 us
    ppermute x3, starting transfers between devices, body(): lax.ppermute(out[i], ('dp', 'tensor'), corner(i // C, i % C))  20.8 us
    all_to_all x1, waiting for transfers between devices, body(): lax.all_to_all(reduced, ('dp', 'tensor'), 0, 0, tiled=True, axis_index_gr...  17.7 us
    all_to_all x1, starting transfers between devices, compress(): lax.all_to_all(after(out, second_seen), 'dp', 0, 0, tiled=True).sum(axis=0)  15.5 us
    all_to_all x1, starting transfers between devices, body(): lax.all_to_all(reduced, ('dp', 'tensor'), 0, 0, tiled=True, axis_index_gr...  12.8 us
    all_to_all x1, blocking collectives, body(): lax.all_to_all(grad, 'tensor', 0, 0, tiled=True, axis_index_groups=X_RINGS)  12.8 us
    ppermute x3, starting transfers between devices, body(): far = lax.ppermute(chunks, 'dp', flipped(step))  12.7 us
  transfers between devices with their start and end apart: 17, of which 9 were waited for; matrix products, arithmetic and copies ran while one was open for 4% of the time, Pallas kernels for 8%

profile of v1, /device:TPU:123, one launch (start us, length us, event | category | flops | bytes accessed | tf_op | source)
XLA Modules:
  0.0 249.6 jit_solution(3427794774204980949)
XLA Ops:
  7.2 1.6 fusion.2
  10.2 4.1 %split.1 = (bf16[128,4096]{1,0:T(8,128)(2,1)S(1)}, bf16[128,4096]{1,0:T(8,128)(2,1)S(1)}, bf16[64,4096]{1,0:T(8,128)(2,1)S(1)}) custom-call(s32[3]{0:T(128)S(1)} %pad_add_fusion.who, bf16[128,8192]{1,0:T(8,128)(2,1)} %x_ref.1, bf16[64,8192]{1,0:T(8,128)(2,1)S(1)} %copy-done.1), custom_call_target="tpu_custom_call" | custom-call | flops 4000000000 | bytes 6000000 | tf_op jit(solution)/shard_map/split/pallas_call | solution.py:229
  16.2 2.6 %collective-permute-start = (bf16[128,4096]{1,0:T(8,128)(2,1)S(1)}, bf16[128,4096]{1,0:T(8,128)(2,1)S(1)}, u32[]{:S(2)}, u32[]{:S(2)}) collective-permute-start(bf16[128,4096]{1,0:T(8,128)(2,1)S(1)} %get-tuple-element.17), channel_id=1, source_target_pairs={{0,8},{8,0},{16,24},{24,16},{32,40},{40,32},{48,56},{56,48},{64,72... | collective-permute-start | bytes 3145736 | tf_op jit(solution)/shard_map/ppermute | solution.py:239
  18.8 8.8 %collective-permute-start.2 = (bf16[1,14,32,128]{3,2,1,0:T(8,128)(2,1)S(1)}, bf16[1,14,32,128]{3,2,1,0:T(8,128)(2,1)S(1)}, u32[]{:S(2)}, u32[]{:S(2)}) collective-permute-start(bf16[1,14,32,128]{3,2,1,0:T(8,128)(2,1)S(1)} %get-tuple-element.32), channel_id=1, source_target_pairs={{0,256},{8,264},{16,272},{24,280},{32,288},{40,296},{48,304},{56,3... | collective-permute-start | bytes 344072 | tf_op jit(solution)/shard_map/ppermute | solution.py:267
  27.6 2.2 collective-permute-start.1
  29.9 6.4 %collective-permute-done.2 = bf16[1,14,32,128]{3,2,1,0:T(8,128)(2,1)S(1)} collective-permute-done((bf16[1,14,32,128]{3,2,1,0:T(8,128)(2,1)S(1)}, bf16[1,14,32,128]{3,2,1,0:T(8,128)(2,1)S(1)}, u32[]{:S(2)}, u32[]{:S(2)}) %collective-permute-start.2) | collective-permute-done | bytes 114720 | tf_op jit(solution)/shard_map/ppermute | solution.py:267
  38.0 1.9 collective-permute-start.3
  44.3 3.0 %compress.1 = f32[64,14,128]{2,1,0:T(8,128)S(1)} custom-call(bf16[128,4096]{1,0:T(8,128)(2,1)S(1)} %copy-done.9, bf16[128,4096]{1,0:T(8,128)(2,1)S(1)} %collective-permute-done.xr_ref.rest_5_.rest_2_, bf16[128,1792]{1,0:T(8,128)(2,1)S(1)} %copy-done.3, bf16[128,1792]{1,0:T(8,128)(2,1)S(1)} %copy-done.5, bf16[64,4096]{1,0:T(8,128)(2,1)S(1)} %copy-done.14, ...), custom_call_target="tpu_custom_call" | custom-call | flops 4000000000 | bytes 6000000 | tf_op jit(solution)/shard_map/compress/pallas_call | solution.py:245
  48.3 4.2 %collective-permute-done.3 = bf16[2,14,32,128]{3,2,1,0:T(8,128)(2,1)S(1)} collective-permute-done((bf16[2,14,32,128]{3,2,1,0:T(8,128)(2,1)S(1)}, bf16[2,14,32,128]{3,2,1,0:T(8,128)(2,1)S(1)}, u32[]{:S(2)}, u32[]{:S(2)}) %collective-permute-start.3) | collective-permute-done | bytes 229408 | tf_op jit(solution)/shard_map/ppermute | solution.py:267
  52.6 1.9 collective-permute-start.4
  56.4 15.5 %all-to-all-start = ((f32[64,14,128]{2,1,0:T(8,128)}), f32[64,14,128]{2,1,0:T(8,128)S(1)}, u32[]{:S(2)}, u32[]{:S(2)}) async-start(f32[64,14,128]{2,1,0:T(8,128)} %broadcast_add_fusion), calls=%async_computation | async-start | bytes 1048576 | tf_op jit(solution)/shard_map/all_to_all | solution.py:255
  72.0 7.6 %collective-permute-start.7 = (bf16[8,7,32,128]{3,2,1,0:T(8,128)(2,1)S(1)}, bf16[8,7,32,128]{3,2,1,0:T(8,128)(2,1)S(1)}, u32[]{:S(2)}, u32[]{:S(2)}) collective-permute-start(bf16[8,7,32,128]{3,2,1,0:T(8,128)(2,1)S(1)} %get-tuple-element.29), channel_id=1, source_target_pairs={{0,48},{8,56},{16,32},{24,40},{32,16},{40,24},{48,0},{56,8},{64,11... | collective-permute-start | bytes 1376264 | tf_op jit(solution)/shard_map/ppermute | solution.py:273
  79.6 1.9 collective-permute-start.5
  81.5 9.4 %collective-permute-done.7 = bf16[8,7,32,128]{3,2,1,0:T(8,128)(2,1)S(1)} collective-permute-done((bf16[8,7,32,128]{3,2,1,0:T(8,128)(2,1)S(1)}, bf16[8,7,32,128]{3,2,1,0:T(8,128)(2,1)S(1)}, u32[]{:S(2)}, u32[]{:S(2)}) %collective-permute-start.7) | collective-permute-done | bytes 458784 | tf_op jit(solution)/shard_map/ppermute | solution.py:273
  91.0 2.4 collective-permute-start.8
  93.4 1.5 collective-permute-done.5
  95.0 3.1 %collective-permute-start.6 = (bf16[16,7,32,128]{3,2,1,0:T(8,128)(2,1)S(1)}, bf16[16,7,32,128]{3,2,1,0:T(8,128)(2,1)}, u32[]{:S(2)}, u32[]{:S(2)}) collective-permute-start(bf16[16,7,32,128]{3,2,1,0:T(8,128)(2,1)S(1)} %pad_maximum_fusion.rest_0_), channel_id=1, source_target_pairs={{0,48},{8,56},{16,32},{24,40},{32,16},{40,24},{48,0},{56,8},{64,11... | collective-permute-start | bytes 2752520 | tf_op jit(solution)/shard_map/ppermute | solution.py:274
  98.1 4.8 %all-to-all-done = f32[64,14,128]{2,1,0:T(8,128)S(1)} async-done(((f32[64,14,128]{2,1,0:T(8,128)}), f32[64,14,128]{2,1,0:T(8,128)S(1)}, u32[]{:S(2)}, u32[]{:S(2)}) %all-to-all-start) | async-done | bytes 458784 | tf_op jit(solution)/shard_map/all_to_all | solution.py:255
  104.1 22.0 %collective-permute-done.8.rest_3_ = bf16[16,7,32,128]{3,2,1,0:T(8,128)(2,1)} collective-permute-done((bf16[16,7,32,128]{3,2,1,0:T(8,128)(2,1)S(1)}, bf16[16,7,32,128]{3,2,1,0:T(8,128)(2,1)}, u32[]{:S(2)}, u32[]{:S(2)}) %collective-permute-start.8) | collective-permute-done | bytes 917536 | tf_op jit(solution)/shard_map/ppermute | solution.py:274
  126.1 10.9 %main.2 = (bf16[4,2,256,256]{3,2,1,0:T(8,128)(2,1)}, f32[128,1792]{1,0:T(8,128)S(1)}, f32[128,1792]{1,0:T(8,128)S(1)}) custom-call(s32[3]{0:T(128)S(1)} %broadcast_add_fusion.3.who, s32[14,32]{1,0:T(8,128)S(1)} %copy-done, bf16[16,7,32,128]{3,2,1,0:T(8,128)(2,1)S(1)} %pad_maximum_fusion.rest_0_, bf16[16,7,32,128]{3,2,1,0:T(8,128)(2,1)} %collective-permute-done.6.rest_1_, ...), custom_call_target="tpu_custom_call" | custom-call | flops 4000000000 | bytes 8000000 | tf_op jit(solution)/shard_map/main/pallas_call | solution.py:284
  138.8 12.8 %all_to_all.20.r_ref = bf16[4,2,256,256]{3,2,1,0:T(8,128)(2,1)S(1)} all-to-all(bf16[4,2,256,256]{3,2,1,0:T(8,128)(2,1)} %get-tuple-element.19), channel_id=1, replica_groups={{0,2,4,6},{1,3,5,7},{8,10,12,14},{9,11,13,15},{16,18,20,22},{17,19,21,2..., dimensions={0} | all-to-all | bytes 2097152 | tf_op jit(solution)/shard_map/all_to_all | solution.py:300
  152.9 4.9 %all-gather.2.cloned.1.call-done = bf16[14,2048,128]{2,1,0:T(8,128)(2,1)} async-done(((bf16[14,32,128]{2,1,0:T(8,128)(2,1)}), bf16[14,2048,128]{2,1,0:T(8,128)(2,1)}) %all-gather.2.cloned.1.call-update) | async-done | bytes 7340048 | tf_op jit(solution)/shard_map/all_gather | solution.py:277
  160.0 12.0 %main.3 = (bf16[4,2,256,256]{3,2,1,0:T(8,128)(2,1)}, f32[128,1792]{1,0:T(8,128)S(1)}, bf16[128,1792]{1,0:T(8,128)(2,1)S(1)}) custom-call(s32[3]{0:T(128)S(1)} %broadcast_add_fusion.2.who, s32[14,32]{1,0:T(8,128)S(1)} %copy-done, bf16[14,32,2,32,128]{4,3,2,1,0:T(8,128)(2,1)} %bitcast.30, bf16[128,4096]{1,0:T(8,128)(2,1)} %copy-done.8, ...), custom_call_target="tpu_custom_call" | custom-call | flops 4000000000 | bytes 8000000 | tf_op jit(solution)/shard_map/main/pallas_call | solution.py:284
  172.8 4.6 %all-to-all-start.2 = ((bf16[4,2,256,256]{3,2,1,0:T(8,128)(2,1)}), bf16[4,2,256,256]{3,2,1,0:T(8,128)(2,1)S(1)}, u32[]{:S(2)}, u32[]{:S(2)}) async-start(bf16[4,2,256,256]{3,2,1,0:T(8,128)(2,1)} %get-tuple-element.24), calls=%async_computation.2 | async-start | bytes 2097152 | tf_op jit(solution)/shard_map/all_to_all | solution.py:300
  179.9 8.4 %collective-permute-start.11 = (bf16[128,256]{1,0:T(8,128)(2,1)S(1)}, bf16[128,256]{1,0:T(8,128)(2,1)S(1)}, u32[]{:S(2)}, u32[]{:S(2)}) collective-permute-start(bf16[128,256]{1,0:T(8,128)(2,1)S(1)} %get-tuple-element.27), channel_id=1, source_target_pairs={{0,1},{1,0},{2,3},{3,2},{4,5},{5,4},{6,7},{7,6},{8,9},{9,8},{10,11... | collective-permute-start | bytes 196616 | tf_op jit(solution)/shard_map/ppermute | solution.py:316
  188.3 10.5 %collective-permute-start.12 = (bf16[128,256]{1,0:T(8,128)(2,1)S(1)}, bf16[128,256]{1,0:T(8,128)(2,1)S(1)}, u32[]{:S(2)}, u32[]{:S(2)}) collective-permute-start(bf16[128,256]{1,0:T(8,128)(2,1)S(1)} %get-tuple-element.28), channel_id=1, source_target_pairs={{0,9},{1,8},{2,11},{3,10},{4,13},{5,12},{6,15},{7,14},{8,1},{9,0},... | collective-permute-start | bytes 196616 | tf_op jit(solution)/shard_map/ppermute | solution.py:316
  198.9 1.9 collective-permute-start.10
  200.8 2.4 collective-permute-start.9
  207.7 1.4 reduce.3
  209.0 12.8 %all-to-all-start.3 = ((bf16[4,128,256]{2,1,0:T(8,128)(2,1)}), bf16[4,128,256]{2,1,0:T(8,128)(2,1)S(1)}, u32[]{:S(2)}, u32[]{:S(2)}) async-start(bf16[4,128,256]{2,1,0:T(8,128)(2,1)} %reduce.3), calls=%async_computation.3 | async-start | bytes 524288 | tf_op jit(solution)/shard_map/all_to_all | solution.py:318
  223.3 17.7 %all-to-all-done.3.refs_4_ = bf16[4,128,256]{2,1,0:T(8,128)(2,1)S(1)} async-done(((bf16[4,128,256]{2,1,0:T(8,128)(2,1)}), bf16[4,128,256]{2,1,0:T(8,128)(2,1)S(1)}, u32[]{:S(2)}, u32[]{:S(2)}) %all-to-all-start.3) | async-done | bytes 262176 | tf_op jit(solution)/shard_map/all_to_all | solution.py:318
  241.1 1.7 final.1
  (76 shorter events, 22.6 us)
Async XLA Ops:
  7.2 150.7 %all-gather.2.cloned.1.call-start = ((), (), s32[]{:S(2)}) async-start(), calls=%async_computation.4 | async-start | bytes 7454720 | tf_op jit(solution)/shard_map/all_gather | solution.py:277
  9.0 1.2 copy-start.1
  10.2 17.4 %copy-start.3 = (bf16[128,1792]{1,0:T(8,128)(2,1)S(1)}, bf16[128,1792]{1,0:T(8,128)(2,1)}, u32[]{:S(2)}) copy-start(bf16[128,1792]{1,0:T(8,128)(2,1)} %rest_3_.1) | copy-start | bytes 1376260
  10.2 19.6 %copy-start = (s32[14,32]{1,0:T(8,128)S(1)}, s32[14,32]{1,0:T(8,128)}, u32[]{:S(2)}) copy-start(s32[14,32]{1,0:T(8,128)} %rows_ref.3) | copy-start | bytes 5380
  14.3 1.1 copy-start.8
  15.4 0.8 copy-start.13
  16.2 24.5 %collective-permute-start = (bf16[128,4096]{1,0:T(8,128)(2,1)S(1)}, bf16[128,4096]{1,0:T(8,128)(2,1)S(1)}, u32[]{:S(2)}, u32[]{:S(2)}) collective-permute-start(bf16[128,4096]{1,0:T(8,128)(2,1)S(1)} %get-tuple-element.17), channel_id=1, source_target_pairs={{0,8},{8,0},{16,24},{24,16},{32,40},{40,32},{48,56},{56,48},{64,72... | collective-permute-start | bytes 3145736 | tf_op jit(solution)/shard_map/ppermute | solution.py:239
  18.8 17.6 %collective-permute-start.2 = (bf16[1,14,32,128]{3,2,1,0:T(8,128)(2,1)S(1)}, bf16[1,14,32,128]{3,2,1,0:T(8,128)(2,1)S(1)}, u32[]{:S(2)}, u32[]{:S(2)}) collective-permute-start(bf16[1,14,32,128]{3,2,1,0:T(8,128)(2,1)S(1)} %get-tuple-element.32), channel_id=1, source_target_pairs={{0,256},{8,264},{16,272},{24,280},{32,288},{40,296},{48,304},{56,3... | collective-permute-start | bytes 344072 | tf_op jit(solution)/shard_map/ppermute | solution.py:267
  27.6 12.3 %collective-permute-start.1 = (bf16[128,1792]{1,0:T(8,128)(2,1)S(1)}, bf16[128,1792]{1,0:T(8,128)(2,1)S(1)}, u32[]{:S(2)}, u32[]{:S(2)}) collective-permute-start(bf16[128,1792]{1,0:T(8,128)(2,1)S(1)} %copy-done.3), channel_id=1, source_target_pairs={{0,8},{8,0},{16,24},{24,16},{32,40},{40,32},{48,56},{56,48},{64,72... | collective-permute-start | bytes 1376264 | tf_op jit(solution)/shard_map/ppermute | solution.py:240
  38.0 14.6 %collective-permute-start.3 = (bf16[2,14,32,128]{3,2,1,0:T(8,128)(2,1)S(1)}, bf16[2,14,32,128]{3,2,1,0:T(8,128)(2,1)S(1)}, u32[]{:S(2)}, u32[]{:S(2)}) collective-permute-start(bf16[2,14,32,128]{3,2,1,0:T(8,128)(2,1)S(1)} %pad_maximum_fusion.3), channel_id=1, source_target_pairs={{0,128},{8,136},{16,144},{24,152},{32,160},{40,168},{48,176},{56,1... | collective-permute-start | bytes 688136 | tf_op jit(solution)/shard_map/ppermute | solution.py:267
  40.7 6.6 %copy-start.2 = (bf16[128,4096]{1,0:T(8,128)(2,1)}, bf16[128,4096]{1,0:T(8,128)(2,1)S(1)}, u32[]{:S(2)}) copy-start(bf16[128,4096]{1,0:T(8,128)(2,1)S(1)} %collective-permute-done.xr_ref.rest_5_.rest_2_) | copy-start | bytes 3145732
  40.7 1.3 copy-start.5
  42.0 1.2 copy-start.9
  43.2 1.0 copy-start.14
  52.6 19.3 %collective-permute-start.4 = (bf16[4,14,32,128]{3,2,1,0:T(8,128)(2,1)S(1)}, bf16[4,14,32,128]{3,2,1,0:T(8,128)(2,1)S(1)}, u32[]{:S(2)}, u32[]{:S(2)}) collective-permute-start(bf16[4,14,32,128]{3,2,1,0:T(8,128)(2,1)S(1)} %maximum_add_fusion), channel_id=1, source_target_pairs={{0,64},{8,72},{16,80},{24,88},{32,96},{40,104},{48,112},{56,120},{... | collective-permute-start | bytes 1376264 | tf_op jit(solution)/shard_map/ppermute | solution.py:267
  56.4 46.5 %all-to-all-start = ((f32[64,14,128]{2,1,0:T(8,128)}), f32[64,14,128]{2,1,0:T(8,128)S(1)}, u32[]{:S(2)}, u32[]{:S(2)}) async-start(f32[64,14,128]{2,1,0:T(8,128)} %broadcast_add_fusion), calls=%async_computation | async-start | bytes 1048576 | tf_op jit(solution)/shard_map/all_to_all | solution.py:255
  72.0 19.0 %collective-permute-start.7 = (bf16[8,7,32,128]{3,2,1,0:T(8,128)(2,1)S(1)}, bf16[8,7,32,128]{3,2,1,0:T(8,128)(2,1)S(1)}, u32[]{:S(2)}, u32[]{:S(2)}) collective-permute-start(bf16[8,7,32,128]{3,2,1,0:T(8,128)(2,1)S(1)} %get-tuple-element.29), channel_id=1, source_target_pairs={{0,48},{8,56},{16,32},{24,40},{32,16},{40,24},{48,0},{56,8},{64,11... | collective-permute-start | bytes 1376264 | tf_op jit(solution)/shard_map/ppermute | solution.py:273
  79.6 15.4 %collective-permute-start.5 = (bf16[8,7,32,128]{3,2,1,0:T(8,128)(2,1)S(1)}, bf16[8,7,32,128]{3,2,1,0:T(8,128)(2,1)S(1)}, u32[]{:S(2)}, u32[]{:S(2)}) collective-permute-start(bf16[8,7,32,128]{3,2,1,0:T(8,128)(2,1)S(1)} %get-tuple-element.30), channel_id=1, source_target_pairs={{0,16},{8,24},{16,0},{24,8},{32,48},{40,56},{48,32},{56,40},{64,80... | collective-permute-start | bytes 1376264 | tf_op jit(solution)/shard_map/ppermute | solution.py:273
  91.0 35.1 %copy-start.15 = (bf16[16,7,32,128]{3,2,1,0:T(8,128)(2,1)}, bf16[16,7,32,128]{3,2,1,0:T(8,128)(2,1)S(1)}, u32[]{:S(2)}) copy-start(bf16[16,7,32,128]{3,2,1,0:T(8,128)(2,1)S(1)} %pad_maximum_fusion.1.rest_2_) | copy-start | bytes 2752516
  91.0 35.1 %collective-permute-start.8 = (bf16[16,7,32,128]{3,2,1,0:T(8,128)(2,1)S(1)}, bf16[16,7,32,128]{3,2,1,0:T(8,128)(2,1)}, u32[]{:S(2)}, u32[]{:S(2)}) collective-permute-start(bf16[16,7,32,128]{3,2,1,0:T(8,128)(2,1)S(1)} %pad_maximum_fusion.1.rest_2_), channel_id=1, source_target_pairs={{0,16},{8,24},{16,0},{24,8},{32,48},{40,56},{48,32},{56,40},{64,80... | collective-permute-start | bytes 2752520 | tf_op jit(solution)/shard_map/ppermute | solution.py:274
  95.0 31.1 %collective-permute-start.6 = (bf16[16,7,32,128]{3,2,1,0:T(8,128)(2,1)S(1)}, bf16[16,7,32,128]{3,2,1,0:T(8,128)(2,1)}, u32[]{:S(2)}, u32[]{:S(2)}) collective-permute-start(bf16[16,7,32,128]{3,2,1,0:T(8,128)(2,1)S(1)} %pad_maximum_fusion.rest_0_), channel_id=1, source_target_pairs={{0,48},{8,56},{16,32},{24,40},{32,16},{40,24},{48,0},{56,8},{64,11... | collective-permute-start | bytes 2752520 | tf_op jit(solution)/shard_map/ppermute | solution.py:274
  137.0 0.9 copy-start.10
  137.9 0.9 copy-start.12
  157.8 1.0 copy-start.6
  158.8 1.2 copy-start.11
  160.0 61.8 %copy-start.16 = (f32[1,1792]{1,0:T(1,128)S(1)}, f32[1,1792]{1,0:T(1,128)}, u32[]{:S(2)}) copy-start(f32[1,1792]{1,0:T(1,128)} %param.11) | copy-start | bytes 21508
  172.8 34.9 %all-to-all-start.2 = ((bf16[4,2,256,256]{3,2,1,0:T(8,128)(2,1)}), bf16[4,2,256,256]{3,2,1,0:T(8,128)(2,1)S(1)}, u32[]{:S(2)}, u32[]{:S(2)}) async-start(bf16[4,2,256,256]{3,2,1,0:T(8,128)(2,1)} %get-tuple-element.24), calls=%async_computation.2 | async-start | bytes 2097152 | tf_op jit(solution)/shard_map/all_to_all | solution.py:300
  179.9 23.3 %collective-permute-start.11 = (bf16[128,256]{1,0:T(8,128)(2,1)S(1)}, bf16[128,256]{1,0:T(8,128)(2,1)S(1)}, u32[]{:S(2)}, u32[]{:S(2)}) collective-permute-start(bf16[128,256]{1,0:T(8,128)(2,1)S(1)} %get-tuple-element.27), channel_id=1, source_target_pairs={{0,1},{1,0},{2,3},{3,2},{4,5},{5,4},{6,7},{7,6},{8,9},{9,8},{10,11... | collective-permute-start | bytes 196616 | tf_op jit(solution)/shard_map/ppermute | solution.py:316
  188.3 16.9 %collective-permute-start.12 = (bf16[128,256]{1,0:T(8,128)(2,1)S(1)}, bf16[128,256]{1,0:T(8,128)(2,1)S(1)}, u32[]{:S(2)}, u32[]{:S(2)}) collective-permute-start(bf16[128,256]{1,0:T(8,128)(2,1)S(1)} %get-tuple-element.28), channel_id=1, source_target_pairs={{0,9},{1,8},{2,11},{3,10},{4,13},{5,12},{6,15},{7,14},{8,1},{9,0},... | collective-permute-start | bytes 196616 | tf_op jit(solution)/shard_map/ppermute | solution.py:316
  198.9 7.5 %collective-permute-start.10 = (bf16[128,256]{1,0:T(8,128)(2,1)S(1)}, bf16[128,256]{1,0:T(8,128)(2,1)S(1)}, u32[]{:S(2)}, u32[]{:S(2)}) collective-permute-start(bf16[128,256]{1,0:T(8,128)(2,1)S(1)} %get-tuple-element.26), channel_id=1, source_target_pairs={{0,8},{1,9},{2,10},{3,11},{4,12},{5,13},{6,14},{7,15},{8,0},{9,1},... | collective-permute-start | bytes 196616 | tf_op jit(solution)/shard_map/ppermute | solution.py:316
  200.8 21.7 %collective-permute-start.9 = (bf16[128,1792]{1,0:T(8,128)(2,1)}, bf16[128,1792]{1,0:T(8,128)(2,1)S(1)}, u32[]{:S(2)}, u32[]{:S(2)}) collective-permute-start(bf16[128,1792]{1,0:T(8,128)(2,1)} %copy-done.7), channel_id=1, source_target_pairs={{0,8},{8,0},{16,24},{24,16},{32,40},{40,32},{48,56},{56,48},{64,72... | collective-permute-start | bytes 1376264 | tf_op jit(solution)/shard_map/ppermute | solution.py:319
  209.0 32.0 %all-to-all-start.3 = ((bf16[4,128,256]{2,1,0:T(8,128)(2,1)}), bf16[4,128,256]{2,1,0:T(8,128)(2,1)S(1)}, u32[]{:S(2)}, u32[]{:S(2)}) async-start(bf16[4,128,256]{2,1,0:T(8,128)(2,1)} %reduce.3), calls=%async_computation.3 | async-start | bytes 524288 | tf_op jit(solution)/shard_map/all_to_all | solution.py:318
  (2 other events, 1.5 us)
Sparse Core Ops, SparseCore 0:
  10.7 147.0 all-gather.1

commit v2 on v1

--- a/solution.py
+++ b/solution.py
@@ -30,12 +30,6 @@
 Z_STEPS = (16, 8, 4)
 Y_STEPS = ((1, 3), (3, 1))
 X_RINGS = [[x * H + h for x in range(X)] for h in range(H)]
-CORNERS = [
-    [place(z, y, core) * (X * H) + x * H + h for h in range(H) for core in range(C)]
-    for z in range(Z)
-    for y in range(Y)
-    for x in range(X)
-]
 
 
 def corner(far_h, far_core):
@@ -179,31 +173,29 @@
             h_ref[:, cols] = out.astype(h_ref.dtype)
 
 
-def reduce_kernel(near, who, r_ref, *outs):
-    core, h_here = who[0], who[2]
-    tokens = outs[0].shape[-2]
+def reduce_kernel(parts, who, *refs):
+    crossings, outs = refs[:parts], refs[parts:]
+    h_here = who[2]
+    tokens = outs[0].shape[1]
     for far_h in range(H):
         for side in range(C):
-            at = pl.ds(side * tokens, tokens) if near else pl.ds(pl.multiple_of((side ^ core) * tokens, tokens), tokens)
-            h = h_here ^ far_h if near else far_h
-            total = r_ref[0, h, at, :].astype(F32)
-            for x in range(1, X):
-                total = total + r_ref[x, h, at, :].astype(F32)
-            if near:
-                outs[far_h * C + side][...] = total.astype(BF16)
-            else:
-                outs[0][far_h * C + side] = total.astype(BF16)
+            at = pl.ds(side * tokens, tokens)
+            for p, r_ref in enumerate(crossings):
+                total = r_ref[0, h_here ^ far_h, at, :].astype(F32)
+                for x in range(1, X):
+                    total = total + r_ref[x, h_here ^ far_h, at, :].astype(F32)
+                outs[far_h * C + side][p] = total.astype(BF16)
 
 
 def final_kernel(parts, half, who, *refs):
-    near, (r,), out_ref = refs[:4], refs[4:-1], refs[-1]
+    near, out_ref = refs[:4], refs[4]
     width = out_ref.shape[1]
-    mine = near[0][...].astype(F32) + near[2][...].astype(F32)
-    other = near[1][...].astype(F32) + near[3][...].astype(F32)
     columns = []
     for side in range(C):
-        columns.append(jnp.where(who[0] == side, mine, other).astype(BF16))
-        columns.append((r[side].astype(F32) + r[C + side].astype(F32)).astype(BF16))
+        for p in range(parts):
+            mine = near[0][p].astype(F32) + near[2][p].astype(F32)
+            other = near[1][p].astype(F32) + near[3][p].astype(F32)
+            columns.append(jnp.where(who[0] == side, mine, other).astype(BF16))
     piece = 128
     group = 2 * parts * piece
     order = regroup(group, parts, half)
@@ -254,7 +246,7 @@
         )(keep, received, grad_hidden, grads_received, proj, after(mask, first_seen))
         return out, lax.all_to_all(after(out, second_seen), "dp", 0, 0, tiled=True).sum(axis=0)
 
-    finals, crossings, acc = [], [], ()
+    crossings, acc = [], ()
     whole = lambda *shape: pl.BlockSpec(shape, lambda i: (0,) * len(shape))
     for p in range(parts):
         own = weight_blocks[:, p * deep : (p + 1) * deep]
@@ -299,30 +291,23 @@
         )(turn, block_rows, *gathered, keep, received, grad_hidden, grads_received, *acc)
         crossed = lax.all_to_all(grad, "tensor", 0, 0, tiled=True, axis_index_groups=X_RINGS)
         crossings.append(crossed)
-    for p in range(parts):
-        near = p == 0
-        piece = sds((tokens, share), BF16)
-        out = pl.pallas_call(
-            functools.partial(reduce_kernel, near),
-            out_shape=(piece,) * 4 if near else (sds((H * C, tokens, share), BF16),),
-            in_specs=[smem, vmem],
-            out_specs=(vmem,) * (4 if near else 1),
-            compiler_params=params(),
-            cost_estimate=cost(10**6, 10**6),
-            name="reduce",
-        )(after(who, *finals[1:]) if p else after(who, grad), crossings[p])
-        reduced = out[0]
-        if near:
-            finals = [out[0]] + [lax.ppermute(out[i], ("dp", "tensor"), corner(i // C, i % C)) for i in range(1, 4)]
-        else:
-            finals.append(lax.all_to_all(reduced, ("dp", "tensor"), 0, 0, tiled=True, axis_index_groups=CORNERS))
+    out = pl.pallas_call(
+        functools.partial(reduce_kernel, parts),
+        out_shape=(sds((parts, tokens, share), BF16),) * 4,
+        in_specs=[smem] + [vmem] * parts,
+        out_specs=(vmem,) * 4,
+        compiler_params=params(),
+        cost_estimate=cost(10**6, 10**6),
+        name="reduce",
+    )(who, *crossings)
+    finals = [out[0]] + [lax.ppermute(out[i], ("dp", "tensor"), corner(i // C, i % C)) for i in range(1, 4)]
     hidden_received = lax.ppermute(acc[1], "dp", OTHER_CORE)
     hidden = (acc[0] + hidden_received.astype(F32)).astype(BF16)
     new_momentum = 0.9 * momentum + summed.reshape(1, units)
     input_grad = pl.pallas_call(
         functools.partial(final_kernel, parts, half),
         out_shape=sds((tokens, width // (X * H)), BF16),
-        in_specs=[smem] + [vmem] * 5,
+        in_specs=[smem] + [vmem] * 4,
         out_specs=vmem,
         compiler_params=params(),
         cost_estimate=cost(10**8, 10**6),

time: 251 us -> 245 us (0.976)
  the two profiles are of different devices: /device:TPU:123 before, /device:TPU:17 now
where the time goes in v2:
time: 245 us; the launch traced here: 244 us
  starting transfers between devices  83 us (34%)
  waiting for transfers between devices  79.6 us (32%)
  Pallas kernels  32.4 us (13%)
  between operations  17.4 us (7%)
  blocking collectives  15.5 us (6%)
  local copies, waits for them, and re-layouts  13.1 us (5%)
  other arithmetic  3.04 us (1%)
    ppermute x3, waiting for transfers between devices, body(): lax.ppermute(out[i], ('dp', 'tensor'), corner(i // C, i % C))  23.4 us
    pallas_call x2, Pallas kernels, body(): pl.pallas_call(functools.partial(main_kernel, first, last), grid=(1,), ou...  22.8 us
    ppermute x3, starting transfers between devices, body(): lax.ppermute(out[i], ('dp', 'tensor'), corner(i // C, i % C))  22 us
    ppermute x2, waiting for transfers between devices, body(): gathered += [some, lax.ppermute(some, 'dp', flipped(y_second))]  21 us
    ppermute x2, starting transfers between devices, body(): some = jnp.concatenate([some, lax.ppermute(some, 'dp', flipped(y_first))])  15.5 us
    all_to_all x1, blocking collectives, body(): lax.all_to_all(grad, 'tensor', 0, 0, tiled=True, axis_index_groups=X_RINGS)  15.5 us
    ppermute x3, waiting for transfers between devices, body(): far = lax.ppermute(chunks, 'dp', flipped(step))  14.8 us
    all_to_all x1, starting transfers between devices, compress(): lax.all_to_all(after(out, second_seen), 'dp', 0, 0, tiled=True).sum(axis=0)  14.2 us
  transfers between devices with their start and end apart: 16, of which 10 were waited for; matrix products, arithmetic and copies ran while one was open for 2% of the time, Pallas kernels for 8%

profile of v2, /device:TPU:17, one launch (start us, length us, event | category | flops | bytes accessed | tf_op | source)
XLA Modules:
  0.0 244.0 jit_solution(13722481686085467542)
XLA Ops:
  7.2 1.6 fusion.2
  10.2 4.1 %split.1 = (bf16[128,4096]{1,0:T(8,128)(2,1)S(1)}, bf16[128,4096]{1,0:T(8,128)(2,1)S(1)}, bf16[64,4096]{1,0:T(8,128)(2,1)S(1)}) custom-call(s32[3]{0:T(128)S(1)} %pad_add_fusion.who, bf16[128,8192]{1,0:T(8,128)(2,1)} %x_ref.1, bf16[64,8192]{1,0:T(8,128)(2,1)S(1)} %copy-done.1), custom_call_target="tpu_custom_call" | custom-call | flops 4000000000 | bytes 6000000 | tf_op jit(solution)/shard_map/split/pallas_call | solution.py:221
  16.2 2.6 %collective-permute-start = (bf16[128,4096]{1,0:T(8,128)(2,1)S(1)}, bf16[128,4096]{1,0:T(8,128)(2,1)S(1)}, u32[]{:S(2)}, u32[]{:S(2)}) collective-permute-start(bf16[128,4096]{1,0:T(8,128)(2,1)S(1)} %get-tuple-element.17), channel_id=1, source_target_pairs={{0,8},{8,0},{16,24},{24,16},{32,40},{40,32},{48,56},{56,48},{64,72... | collective-permute-start | bytes 3145736 | tf_op jit(solution)/shard_map/ppermute | solution.py:231
  18.7 8.8 %collective-permute-start.2 = (bf16[1,14,32,128]{3,2,1,0:T(8,128)(2,1)S(1)}, bf16[1,14,32,128]{3,2,1,0:T(8,128)(2,1)S(1)}, u32[]{:S(2)}, u32[]{:S(2)}) collective-permute-start(bf16[1,14,32,128]{3,2,1,0:T(8,128)(2,1)S(1)} %get-tuple-element.32), channel_id=1, source_target_pairs={{0,256},{8,264},{16,272},{24,280},{32,288},{40,296},{48,304},{56,3... | collective-permute-start | bytes 344072 | tf_op jit(solution)/shard_map/ppermute | solution.py:259
  27.6 2.2 collective-permute-start.1
  29.9 8.5 %collective-permute-done.2 = bf16[1,14,32,128]{3,2,1,0:T(8,128)(2,1)S(1)} collective-permute-done((bf16[1,14,32,128]{3,2,1,0:T(8,128)(2,1)S(1)}, bf16[1,14,32,128]{3,2,1,0:T(8,128)(2,1)S(1)}, u32[]{:S(2)}, u32[]{:S(2)}) %collective-permute-start.2) | collective-permute-done | bytes 114720 | tf_op jit(solution)/shard_map/ppermute | solution.py:259
  40.0 1.9 collective-permute-start.3
  42.0 1.8 copy-done.8
  44.8 3.0 %compress.1 = f32[64,14,128]{2,1,0:T(8,128)S(1)} custom-call(bf16[128,4096]{1,0:T(8,128)(2,1)S(1)} %copy-done.8, bf16[128,4096]{1,0:T(8,128)(2,1)S(1)} %collective-permute-done.xr_ref.rest_5_.rest_2_, bf16[128,1792]{1,0:T(8,128)(2,1)S(1)} %copy-done.3, bf16[128,1792]{1,0:T(8,128)(2,1)S(1)} %collective-permute-done.1.gr_ref.rest_7_.rest_4_, ...), custom_call_target="tpu_custom_call" | custom-call | flops 4000000000 | bytes 6000000 | tf_op jit(solution)/shard_map/compress/pallas_call | solution.py:237
  48.9 6.3 %collective-permute-done.3 = bf16[2,14,32,128]{3,2,1,0:T(8,128)(2,1)S(1)} collective-permute-done((bf16[2,14,32,128]{3,2,1,0:T(8,128)(2,1)S(1)}, bf16[2,14,32,128]{3,2,1,0:T(8,128)(2,1)S(1)}, u32[]{:S(2)}, u32[]{:S(2)}) %collective-permute-start.3) | collective-permute-done | bytes 229408 | tf_op jit(solution)/shard_map/ppermute | solution.py:259
  55.3 1.9 collective-permute-start.4
  59.1 14.2 %all-to-all-start = ((f32[64,14,128]{2,1,0:T(8,128)}), f32[64,14,128]{2,1,0:T(8,128)S(1)}, u32[]{:S(2)}, u32[]{:S(2)}) async-start(f32[64,14,128]{2,1,0:T(8,128)} %broadcast_add_fusion), calls=%async_computation | async-start | bytes 1048576 | tf_op jit(solution)/shard_map/all_to_all | solution.py:247
  73.4 2.2 collective-permute-start.7
  75.6 13.3 %collective-permute-start.5 = (bf16[8,7,32,128]{3,2,1,0:T(8,128)(2,1)S(1)}, bf16[8,7,32,128]{3,2,1,0:T(8,128)(2,1)S(1)}, u32[]{:S(2)}, u32[]{:S(2)}) collective-permute-start(bf16[8,7,32,128]{3,2,1,0:T(8,128)(2,1)S(1)} %get-tuple-element.30), channel_id=1, source_target_pairs={{0,16},{8,24},{16,0},{24,8},{32,48},{40,56},{48,32},{56,40},{64,80... | collective-permute-start | bytes 1376264 | tf_op jit(solution)/shard_map/ppermute | solution.py:265
  88.9 8.4 %collective-permute-done.7 = bf16[8,7,32,128]{3,2,1,0:T(8,128)(2,1)S(1)} collective-permute-done((bf16[8,7,32,128]{3,2,1,0:T(8,128)(2,1)S(1)}, bf16[8,7,32,128]{3,2,1,0:T(8,128)(2,1)S(1)}, u32[]{:S(2)}, u32[]{:S(2)}) %collective-permute-start.7) | collective-permute-done | bytes 458784 | tf_op jit(solution)/shard_map/ppermute | solution.py:265
  97.4 1.9 collective-permute-start.8
  99.3 3.1 %collective-permute-done.5 = bf16[8,7,32,128]{3,2,1,0:T(8,128)(2,1)S(1)} collective-permute-done((bf16[8,7,32,128]{3,2,1,0:T(8,128)(2,1)S(1)}, bf16[8,7,32,128]{3,2,1,0:T(8,128)(2,1)S(1)}, u32[]{:S(2)}, u32[]{:S(2)}) %collective-permute-start.5) | collective-permute-done | bytes 458784 | tf_op jit(solution)/shard_map/ppermute | solution.py:265
  102.5 2.1 collective-permute-start.6
  104.6 2.3 all-to-all-done
  108.1 21.0 %collective-permute-done.8.rest_3_ = bf16[16,7,32,128]{3,2,1,0:T(8,128)(2,1)} collective-permute-done((bf16[16,7,32,128]{3,2,1,0:T(8,128)(2,1)S(1)}, bf16[16,7,32,128]{3,2,1,0:T(8,128)(2,1)}, u32[]{:S(2)}, u32[]{:S(2)}) %collective-permute-start.8) | collective-permute-done | bytes 917536 | tf_op jit(solution)/shard_map/ppermute | solution.py:266
  129.2 10.8 %main.2 = (bf16[4,2,256,256]{3,2,1,0:T(8,128)(2,1)}, f32[128,1792]{1,0:T(8,128)S(1)}, f32[128,1792]{1,0:T(8,128)S(1)}) custom-call(s32[3]{0:T(128)S(1)} %broadcast_add_fusion.2.who, s32[14,32]{1,0:T(8,128)S(1)} %copy-done, bf16[16,7,32,128]{3,2,1,0:T(8,128)(2,1)S(1)} %pad_maximum_fusion.rest_0_, bf16[16,7,32,128]{3,2,1,0:T(8,128)(2,1)} %collective-permute-done.6.rest_1_, ...), custom_call_target="tpu_custom_call" | custom-call | flops 4000000000 | bytes 8000000 | tf_op jit(solution)/shard_map/main/pallas_call | solution.py:276
  140.9 15.5 %all_to_all.15.refs_0_ = bf16[4,2,256,256]{3,2,1,0:T(8,128)(2,1)S(1)} all-to-all(bf16[4,2,256,256]{3,2,1,0:T(8,128)(2,1)} %get-tuple-element.19), channel_id=1, replica_groups={{0,2,4,6},{1,3,5,7},{8,10,12,14},{9,11,13,15},{16,18,20,22},{17,19,21,2..., dimensions={0} | all-to-all | bytes 2097152 | tf_op jit(solution)/shard_map/all_to_all | solution.py:292
  157.6 1.8 all-gather.2.cloned.1.call-done
  160.4 12.0 %main.3 = (bf16[4,2,256,256]{3,2,1,0:T(8,128)(2,1)}, f32[128,1792]{1,0:T(8,128)S(1)}, bf16[128,1792]{1,0:T(8,128)(2,1)S(1)}) custom-call(s32[3]{0:T(128)S(1)} %broadcast_add_fusion.1.who, s32[14,32]{1,0:T(8,128)S(1)} %copy-done, bf16[14,32,2,32,128]{4,3,2,1,0:T(8,128)(2,1)} %bitcast.22, bf16[128,4096]{1,0:T(8,128)(2,1)} %copy-done.7, ...), custom_call_target="tpu_custom_call" | custom-call | flops 4000000000 | bytes 8000000 | tf_op jit(solution)/shard_map/main/pallas_call | solution.py:276
  173.1 4.2 %all-to-all-start.2 = ((bf16[4,2,256,256]{3,2,1,0:T(8,128)(2,1)}), bf16[4,2,256,256]{3,2,1,0:T(8,128)(2,1)S(1)}, u32[]{:S(2)}, u32[]{:S(2)}) async-start(bf16[4,2,256,256]{3,2,1,0:T(8,128)(2,1)} %get-tuple-element.24), calls=%async_computation.2 | async-start | bytes 2097152 | tf_op jit(solution)/shard_map/all_to_all | solution.py:292
  177.3 5.7 %collective-permute-start.9 = (bf16[128,1792]{1,0:T(8,128)(2,1)}, bf16[128,1792]{1,0:T(8,128)(2,1)S(1)}, u32[]{:S(2)}, u32[]{:S(2)}) collective-permute-start(bf16[128,1792]{1,0:T(8,128)(2,1)} %copy-done.6), channel_id=1, source_target_pairs={{0,8},{8,0},{16,24},{24,16},{32,40},{40,32},{48,56},{56,48},{64,72... | collective-permute-start | bytes 1376264 | tf_op jit(solution)/shard_map/ppermute | solution.py:304
  183.6 4.8 %all-to-all-done.2.refs_1_ = bf16[4,2,256,256]{3,2,1,0:T(8,128)(2,1)S(1)} async-done(((bf16[4,2,256,256]{3,2,1,0:T(8,128)(2,1)}), bf16[4,2,256,256]{3,2,1,0:T(8,128)(2,1)S(1)}, u32[]{:S(2)}, u32[]{:S(2)}) %all-to-all-start.2) | async-done | bytes 1048608 | tf_op jit(solution)/shard_map/all_to_all | solution.py:292
  189.2 6.9 %collective-permute-start.10 = (bf16[2,128,256]{2,1,0:T(8,128)(2,1)S(1)}, bf16[2,128,256]{2,1,0:T(8,128)(2,1)S(1)}, u32[]{:S(2)}, u32[]{:S(2)}) collective-permute-start(bf16[2,128,256]{2,1,0:T(8,128)(2,1)S(1)} %get-tuple-element.26), channel_id=1, source_target_pairs={{0,8},{1,9},{2,10},{3,11},{4,12},{5,13},{6,14},{7,15},{8,0},{9,1},... | collective-permute-start | bytes 393224 | tf_op jit(solution)/shard_map/ppermute | solution.py:303
  196.1 13.2 %collective-permute-start.11 = (bf16[2,128,256]{2,1,0:T(8,128)(2,1)S(1)}, bf16[2,128,256]{2,1,0:T(8,128)(2,1)S(1)}, u32[]{:S(2)}, u32[]{:S(2)}) collective-permute-start(bf16[2,128,256]{2,1,0:T(8,128)(2,1)S(1)} %get-tuple-element.27), channel_id=1, source_target_pairs={{0,1},{1,0},{2,3},{3,2},{4,5},{5,4},{6,7},{7,6},{8,9},{9,8},{10,11... | collective-permute-start | bytes 393224 | tf_op jit(solution)/shard_map/ppermute | solution.py:303
  209.3 1.9 collective-permute-start.12
  213.1 22.3 %collective-permute-done.12.refs_3_ = bf16[2,128,256]{2,1,0:T(8,128)(2,1)S(1)} collective-permute-done((bf16[2,128,256]{2,1,0:T(8,128)(2,1)S(1)}, bf16[2,128,256]{2,1,0:T(8,128)(2,1)S(1)}, u32[]{:S(2)}, u32[]{:S(2)}) %collective-permute-start.12) | collective-permute-done | bytes 131104 | tf_op jit(solution)/shard_map/ppermute | solution.py:303
  235.5 1.7 final.1
  (61 shorter events, 14.7 us)
Async XLA Ops:
  7.2 152.2 %all-gather.2.cloned.1.call-start = ((), (), s32[]{:S(2)}) async-start(), calls=%async_computation.3 | async-start | bytes 7454720 | tf_op jit(solution)/shard_map/all_gather | solution.py:269
  9.0 1.2 copy-start.1
  10.2 17.4 %copy-start.3 = (bf16[128,1792]{1,0:T(8,128)(2,1)S(1)}, bf16[128,1792]{1,0:T(8,128)(2,1)}, u32[]{:S(2)}) copy-start(bf16[128,1792]{1,0:T(8,128)(2,1)} %rest_3_.1) | copy-start | bytes 1376260
  10.2 19.6 %copy-start = (s32[14,32]{1,0:T(8,128)S(1)}, s32[14,32]{1,0:T(8,128)}, u32[]{:S(2)}) copy-start(s32[14,32]{1,0:T(8,128)} %rows_ref.3) | copy-start | bytes 5380
  14.3 1.1 copy-start.7
  15.4 0.8 copy-start.10
  16.2 25.8 %collective-permute-start = (bf16[128,4096]{1,0:T(8,128)(2,1)S(1)}, bf16[128,4096]{1,0:T(8,128)(2,1)S(1)}, u32[]{:S(2)}, u32[]{:S(2)}) collective-permute-start(bf16[128,4096]{1,0:T(8,128)(2,1)S(1)} %get-tuple-element.17), channel_id=1, source_target_pairs={{0,8},{8,0},{16,24},{24,16},{32,40},{40,32},{48,56},{56,48},{64,72... | collective-permute-start | bytes 3145736 | tf_op jit(solution)/shard_map/ppermute | solution.py:231
  18.7 19.7 %collective-permute-start.2 = (bf16[1,14,32,128]{3,2,1,0:T(8,128)(2,1)S(1)}, bf16[1,14,32,128]{3,2,1,0:T(8,128)(2,1)S(1)}, u32[]{:S(2)}, u32[]{:S(2)}) collective-permute-start(bf16[1,14,32,128]{3,2,1,0:T(8,128)(2,1)S(1)} %get-tuple-element.32), channel_id=1, source_target_pairs={{0,256},{8,264},{16,272},{24,280},{32,288},{40,296},{48,304},{56,3... | collective-permute-start | bytes 344072 | tf_op jit(solution)/shard_map/ppermute | solution.py:259
  27.6 14.4 %collective-permute-start.1 = (bf16[128,1792]{1,0:T(8,128)(2,1)S(1)}, bf16[128,1792]{1,0:T(8,128)(2,1)S(1)}, u32[]{:S(2)}, u32[]{:S(2)}) collective-permute-start(bf16[128,1792]{1,0:T(8,128)(2,1)S(1)} %copy-done.3), channel_id=1, source_target_pairs={{0,8},{8,0},{16,24},{24,16},{32,40},{40,32},{48,56},{56,48},{64,72... | collective-permute-start | bytes 1376264 | tf_op jit(solution)/shard_map/ppermute | solution.py:232
  40.0 15.2 %collective-permute-start.3 = (bf16[2,14,32,128]{3,2,1,0:T(8,128)(2,1)S(1)}, bf16[2,14,32,128]{3,2,1,0:T(8,128)(2,1)S(1)}, u32[]{:S(2)}, u32[]{:S(2)}) collective-permute-start(bf16[2,14,32,128]{3,2,1,0:T(8,128)(2,1)S(1)} %pad_maximum_fusion.3), channel_id=1, source_target_pairs={{0,128},{8,136},{16,144},{24,152},{32,160},{40,168},{48,176},{56,1... | collective-permute-start | bytes 688136 | tf_op jit(solution)/shard_map/ppermute | solution.py:259
  42.0 87.2 %copy-start.4 = (bf16[128,1792]{1,0:T(8,128)(2,1)}, bf16[128,1792]{1,0:T(8,128)(2,1)S(1)}, u32[]{:S(2)}) copy-start(bf16[128,1792]{1,0:T(8,128)(2,1)S(1)} %collective-permute-done.1.gr_ref.rest_7_.rest_4_) | copy-start | bytes 1376260
  42.0 5.8 %copy-start.2 = (bf16[128,4096]{1,0:T(8,128)(2,1)}, bf16[128,4096]{1,0:T(8,128)(2,1)S(1)}, u32[]{:S(2)}) copy-start(bf16[128,4096]{1,0:T(8,128)(2,1)S(1)} %collective-permute-done.xr_ref.rest_5_.rest_2_) | copy-start | bytes 3145732
  42.0 1.8 copy-start.8
  43.8 1.0 copy-start.11
  55.3 18.0 %collective-permute-start.4 = (bf16[4,14,32,128]{3,2,1,0:T(8,128)(2,1)S(1)}, bf16[4,14,32,128]{3,2,1,0:T(8,128)(2,1)S(1)}, u32[]{:S(2)}, u32[]{:S(2)}) collective-permute-start(bf16[4,14,32,128]{3,2,1,0:T(8,128)(2,1)S(1)} %maximum_add_fusion), channel_id=1, source_target_pairs={{0,64},{8,72},{16,80},{24,88},{32,96},{40,104},{48,112},{56,120},{... | collective-permute-start | bytes 1376264 | tf_op jit(solution)/shard_map/ppermute | solution.py:259
  59.1 47.8 %all-to-all-start = ((f32[64,14,128]{2,1,0:T(8,128)}), f32[64,14,128]{2,1,0:T(8,128)S(1)}, u32[]{:S(2)}, u32[]{:S(2)}) async-start(f32[64,14,128]{2,1,0:T(8,128)} %broadcast_add_fusion), calls=%async_computation | async-start | bytes 1048576 | tf_op jit(solution)/shard_map/all_to_all | solution.py:247
  73.4 23.9 %collective-permute-start.7 = (bf16[8,7,32,128]{3,2,1,0:T(8,128)(2,1)S(1)}, bf16[8,7,32,128]{3,2,1,0:T(8,128)(2,1)S(1)}, u32[]{:S(2)}, u32[]{:S(2)}) collective-permute-start(bf16[8,7,32,128]{3,2,1,0:T(8,128)(2,1)S(1)} %get-tuple-element.29), channel_id=1, source_target_pairs={{0,48},{8,56},{16,32},{24,40},{32,16},{40,24},{48,0},{56,8},{64,11... | collective-permute-start | bytes 1376264 | tf_op jit(solution)/shard_map/ppermute | solution.py:265
  75.6 26.8 %collective-permute-start.5 = (bf16[8,7,32,128]{3,2,1,0:T(8,128)(2,1)S(1)}, bf16[8,7,32,128]{3,2,1,0:T(8,128)(2,1)S(1)}, u32[]{:S(2)}, u32[]{:S(2)}) collective-permute-start(bf16[8,7,32,128]{3,2,1,0:T(8,128)(2,1)S(1)} %get-tuple-element.30), channel_id=1, source_target_pairs={{0,16},{8,24},{16,0},{24,8},{32,48},{40,56},{48,32},{56,40},{64,80... | collective-permute-start | bytes 1376264 | tf_op jit(solution)/shard_map/ppermute | solution.py:265
  97.4 31.8 %copy-start.12 = (bf16[16,7,32,128]{3,2,1,0:T(8,128)(2,1)}, bf16[16,7,32,128]{3,2,1,0:T(8,128)(2,1)S(1)}, u32[]{:S(2)}) copy-start(bf16[16,7,32,128]{3,2,1,0:T(8,128)(2,1)S(1)} %pad_maximum_fusion.1.rest_2_) | copy-start | bytes 2752516
  97.4 31.8 %collective-permute-start.8 = (bf16[16,7,32,128]{3,2,1,0:T(8,128)(2,1)S(1)}, bf16[16,7,32,128]{3,2,1,0:T(8,128)(2,1)}, u32[]{:S(2)}, u32[]{:S(2)}) collective-permute-start(bf16[16,7,32,128]{3,2,1,0:T(8,128)(2,1)S(1)} %pad_maximum_fusion.1.rest_2_), channel_id=1, source_target_pairs={{0,16},{8,24},{16,0},{24,8},{32,48},{40,56},{48,32},{56,40},{64,80... | collective-permute-start | bytes 2752520 | tf_op jit(solution)/shard_map/ppermute | solution.py:266
  102.5 26.6 %collective-permute-start.6 = (bf16[16,7,32,128]{3,2,1,0:T(8,128)(2,1)S(1)}, bf16[16,7,32,128]{3,2,1,0:T(8,128)(2,1)}, u32[]{:S(2)}, u32[]{:S(2)}) collective-permute-start(bf16[16,7,32,128]{3,2,1,0:T(8,128)(2,1)S(1)} %pad_maximum_fusion.rest_0_), channel_id=1, source_target_pairs={{0,48},{8,56},{16,32},{24,40},{32,16},{40,24},{48,0},{56,8},{64,11... | collective-permute-start | bytes 2752520 | tf_op jit(solution)/shard_map/ppermute | solution.py:266
  140.0 0.9 copy-start.9
  159.4 1.0 copy-start.5
  160.4 22.6 %copy-start.13 = (f32[1,1792]{1,0:T(1,128)S(1)}, f32[1,1792]{1,0:T(1,128)}, u32[]{:S(2)}) copy-start(f32[1,1792]{1,0:T(1,128)} %param.11) | copy-start | bytes 21508
  172.4 0.8 copy-start.6
  173.1 15.3 %all-to-all-start.2 = ((bf16[4,2,256,256]{3,2,1,0:T(8,128)(2,1)}), bf16[4,2,256,256]{3,2,1,0:T(8,128)(2,1)S(1)}, u32[]{:S(2)}, u32[]{:S(2)}) async-start(bf16[4,2,256,256]{3,2,1,0:T(8,128)(2,1)} %get-tuple-element.24), calls=%async_computation.2 | async-start | bytes 2097152 | tf_op jit(solution)/shard_map/all_to_all | solution.py:292
  177.3 33.9 %collective-permute-start.9 = (bf16[128,1792]{1,0:T(8,128)(2,1)}, bf16[128,1792]{1,0:T(8,128)(2,1)S(1)}, u32[]{:S(2)}, u32[]{:S(2)}) collective-permute-start(bf16[128,1792]{1,0:T(8,128)(2,1)} %copy-done.6), channel_id=1, source_target_pairs={{0,8},{8,0},{16,24},{24,16},{32,40},{40,32},{48,56},{56,48},{64,72... | collective-permute-start | bytes 1376264 | tf_op jit(solution)/shard_map/ppermute | solution.py:304
  189.2 22.9 %collective-permute-start.10 = (bf16[2,128,256]{2,1,0:T(8,128)(2,1)S(1)}, bf16[2,128,256]{2,1,0:T(8,128)(2,1)S(1)}, u32[]{:S(2)}, u32[]{:S(2)}) collective-permute-start(bf16[2,128,256]{2,1,0:T(8,128)(2,1)S(1)} %get-tuple-element.26), channel_id=1, source_target_pairs={{0,8},{1,9},{2,10},{3,11},{4,12},{5,13},{6,14},{7,15},{8,0},{9,1},... | collective-permute-start | bytes 393224 | tf_op jit(solution)/shard_map/ppermute | solution.py:303
  196.1 17.0 %collective-permute-start.11 = (bf16[2,128,256]{2,1,0:T(8,128)(2,1)S(1)}, bf16[2,128,256]{2,1,0:T(8,128)(2,1)S(1)}, u32[]{:S(2)}, u32[]{:S(2)}) collective-permute-start(bf16[2,128,256]{2,1,0:T(8,128)(2,1)S(1)} %get-tuple-element.27), channel_id=1, source_target_pairs={{0,1},{1,0},{2,3},{3,2},{4,5},{5,4},{6,7},{7,6},{8,9},{9,8},{10,11... | collective-permute-start | bytes 393224 | tf_op jit(solution)/shard_map/ppermute | solution.py:303
  209.3 26.2 %collective-permute-start.12 = (bf16[2,128,256]{2,1,0:T(8,128)(2,1)S(1)}, bf16[2,128,256]{2,1,0:T(8,128)(2,1)S(1)}, u32[]{:S(2)}, u32[]{:S(2)}) collective-permute-start(bf16[2,128,256]{2,1,0:T(8,128)(2,1)S(1)} %get-tuple-element.28), channel_id=1, source_target_pairs={{0,9},{1,8},{2,11},{3,10},{4,13},{5,12},{6,15},{7,14},{8,1},{9,0},... | collective-permute-start | bytes 393224 | tf_op jit(solution)/shard_map/ppermute | solution.py:303
Sparse Core Ops, SparseCore 0:
  10.7 148.5 all-gather.1
